TPU v7x, 32 devices: a whole 2x2x4 slice. The times are simulated.
32 devices in a mesh: lat: 8 (over z, x), deg: 4 (over y, core).
Axes of the slice: x: 2, y: 2, z: 4, core: 2. Of those that a mesh axis runs over, the one named last changes fastest.
Arguments:
- eta_tl: float32 [64, 10752], P('lat'), may hold values from -6 to 6
- vel_tl: float32 [2, 64, 10752], P(None, 'lat'), may hold values from -6 to 6
- eta_adj: float32 [64, 10752], P('lat'), may hold values from -6 to 6
- vel_adj: float32 [2, 64, 10752], P(None, 'lat'), may hold values from -6 to 6
- depth: float32 [64, 10752], P('lat'), may hold values from 0.2 to 1
- drag: float32 [64, 10752], P('lat'), may hold values from 0.01 to 0.3
- ocean: int32 [64, 10752], P('lat'), may hold values 0 or 1
- basis: bfloat16 [1024, 64, 1024], P('lat', None, 'deg'), may hold values from -5 to 5
- love: float32 [1024], P('deg'), may hold values from 0.05 to 0.5
Outputs:
- eta_tl_out: float32 [64, 10752], P('lat')
- vel_tl_out: float32 [2, 64, 10752], P(None, 'lat')
- eta_adj_out: float32 [64, 10752], P('lat')
- vel_adj_out: float32 [2, 64, 10752], P(None, 'lat')
All inputs are finite; a program needn't handle non-finite values. No bound on the sum of `ocean` on one device may be relied on, other than what follows from the above.
Results may differ from a plain program's by a relative error of at most 0.02.
Values may be sent and summed in bfloat16 or wider, within the bound.
A program may use at most 320 MiB of HBM per device.

v0:
```python
import jax
import jax.numpy as jnp
from jax import lax
from jax.sharding import PartitionSpec as P

STEPS = 2
kappa_x = 0.3
kappa_y = 0.4


def as_sent(value):
    return jax.tree.map(lambda a: a.astype(jnp.bfloat16) if a.dtype == jnp.float32 else a, value)


def passed_along(value, axis, by):
    length = lax.axis_size(axis)
    pairs = [(i, i + by) for i in range(length) if 0 <= i + by < length]
    return lax.ppermute(value, axis, pairs)


def trig_table(orders, lon_count):
    lon_cells = jnp.arange(lon_count, dtype=jnp.int32)
    phase_index = lon_cells[:, None] * orders[None, :] % lon_count
    angles = phase_index.astype(jnp.float32) * (2.0 * jnp.pi / lon_count)
    return jnp.concatenate([jnp.cos(angles), jnp.sin(angles)], axis=1).astype(jnp.bfloat16)


def order_factor(orders):
    return jnp.where(orders == 0, 1.0, 2.0).astype(jnp.bfloat16)


def analyse(stacked, analysis_weight, table_now, order_count):
    row_count = stacked.shape[1]
    lon_count = stacked.shape[2]
    flat_rows = stacked.astype(jnp.bfloat16).reshape(2 * row_count, lon_count)
    spectra = lax.dot_general(
        table_now, flat_rows, (((0,), (1,)), ((), ())), preferred_element_type=jnp.float32
    )
    spectra = spectra.reshape(2, order_count, 2, row_count) * (1.0 / lon_count)
    return (spectra * analysis_weight[None, None, :, :]).astype(jnp.bfloat16)


def legendre(spectra, basis, love):
    coeffs = jnp.einsum("cmfi,mil->cmfl", spectra, basis, preferred_element_type=jnp.float32)
    scaled = (coeffs * love[None, None, None, :]).astype(jnp.bfloat16)
    return jnp.einsum("cmfl,mil->cmfi", scaled, basis, preferred_element_type=jnp.float32)


def synthesise(coeffs, factors, table_now, output_weight):
    order_count = coeffs.shape[1]
    row_count = coeffs.shape[3]
    scaled = (coeffs * factors[None, :, None, None]).reshape(2 * order_count, 2 * row_count)
    grid_out = lax.dot_general(
        scaled, table_now, (((0,), (1,)), ((), ())), preferred_element_type=jnp.float32
    )
    return grid_out.reshape(2, row_count, -1) * output_weight[:, :, None]


def from_north(edge_row):
    return passed_along(as_sent(edge_row), "lat", -1).astype(edge_row.dtype)


def from_south(edge_row):
    return passed_along(as_sent(edge_row), "lat", 1).astype(edge_row.dtype)


def on_device(eta_tl, vel_tl, eta_adj, vel_adj, depth, drag, ocean, basis, love):
    row_count = eta_tl.shape[0]
    lon_count = eta_tl.shape[1]
    lat_count = lax.axis_size("lat")
    total_rows = row_count * lat_count
    first_row = lax.axis_index("lat") * row_count
    indices = first_row + jnp.arange(row_count, dtype=jnp.int32)
    latitude = (indices.astype(jnp.float32) + 0.5) * (jnp.pi / total_rows) - 0.5 * jnp.pi
    cosine = jnp.cos(latitude)
    quad_weight = jnp.pi / total_rows * cosine
    east_factor = (kappa_x / (0.5 + 0.5 * cosine))[:, None]
    wet_mask = ocean.astype(jnp.float32)
    north_depth, north_wet = (
        passed_along(depth[:1].astype(jnp.bfloat16), "lat", -1).astype(jnp.float32),
        passed_along(wet_mask[:1].astype(jnp.bfloat16), "lat", -1).astype(jnp.float32),
    )
    depth_up = jnp.concatenate([depth[1:], north_depth], 0)
    wet_up = jnp.concatenate([wet_mask[1:], north_wet], 0)
    mask_u = wet_mask * jnp.roll(wet_mask, -1, 1)
    mask_v = wet_mask * wet_up
    depth_u = 0.5 * (depth + jnp.roll(depth, -1, 1))
    depth_v = 0.5 * (depth + depth_up)
    retain = 1.0 - drag
    ones_weight = jnp.ones_like(quad_weight)
    analysis_weight = jnp.stack([quad_weight, ones_weight])
    output_weight = jnp.stack([ones_weight, quad_weight])
    owned_count = basis.shape[0]
    order_total = owned_count * lat_count
    full_orders = jnp.arange(order_total, dtype=jnp.int32)
    full_table = trig_table(full_orders, lon_count)
    full_factor = order_factor(full_orders)
    state_eta, state_vel = (eta_tl, vel_tl)
    back_eta, back_vel = (eta_adj, vel_adj)
    for step_index in range(STEPS):
        flux_east = east_factor * wet_mask * back_eta
        flux_north = kappa_y * wet_mask * back_eta
        north_up = jnp.concatenate([flux_north[1:], from_north(flux_north[:1])], 0)
        p_term = mask_u * (back_vel[0] + depth_u * (jnp.roll(flux_east, -1, 1) - flux_east))
        q_term = mask_v * (back_vel[1] + depth_v * (north_up - flux_north))
        q_down = jnp.concatenate([from_south(q_term[-1:]), q_term[:-1]], 0)
        flux_p = east_factor * p_term
        psi_bar = flux_p - jnp.roll(flux_p, 1, 1) + kappa_y * (q_term - q_down)
        spectra = analyse(jnp.stack([state_eta, psi_bar]), analysis_weight, full_table, order_total)
        owned_rows = lax.all_to_all(spectra, "lat", split_axis=1, concat_axis=3, tiled=True)
        partial_value = legendre(owned_rows, basis, love)
        total_sum = lax.psum(partial_value.astype(jnp.bfloat16), "deg")
        banded = lax.all_to_all(total_sum, "lat", split_axis=3, concat_axis=1, tiled=True)
        loads = synthesise(banded, full_factor, full_table, output_weight)
        psi_now = state_eta - loads[0]
        psi_up = jnp.concatenate([psi_now[1:], from_north(psi_now[:1])], 0)
        new_u = mask_u * (
            retain * state_vel[0] - east_factor * (jnp.roll(psi_now, -1, 1) - psi_now)
        )
        new_v = mask_v * (retain * state_vel[1] - kappa_y * (psi_up - psi_now))
        flux_x = depth_u * new_u
        flux_y = depth_v * new_v
        flux_down = jnp.concatenate([from_south(flux_y[-1:]), flux_y[:-1]], 0)
        state_eta = state_eta - wet_mask * (
            east_factor * (flux_x - jnp.roll(flux_x, 1, 1)) + kappa_y * (flux_y - flux_down)
        )
        state_vel = jnp.stack([new_u, new_v])
        back_eta = back_eta + psi_bar - loads[1]
        back_vel = jnp.stack([retain * p_term, retain * q_term])
    return (state_eta, state_vel, back_eta, back_vel)


def solution(mesh):
    in_specs = (
        P("lat", None),
        P(None, "lat", None),
        P("lat", None),
        P(None, "lat", None),
        P("lat", None),
        P("lat", None),
        P("lat", None),
        P("lat", None, "deg"),
        P("deg"),
    )
    out_specs = (P("lat", None), P(None, "lat", None), P("lat", None), P(None, "lat", None))
    return jax.shard_map(
        on_device, mesh=mesh, in_specs=in_specs, out_specs=out_specs, check_vma=False
    )
```

profile of v0, /device:TPU:0, one launch (start us, length us, event | category | flops | bytes accessed | tf_op | source)
XLA Modules:
  0.0 552.0 jit_solution(11705418563088993422)
XLA Ops:
  7.3 1.2 multiply_multiply_fusion.3
  8.5 1.3 collective-permute-start.2
  9.8 1.0 slice.281
  10.8 1.3 collective-permute-start.1
  12.1 1.0 convert_element_type.110
  13.2 1.3 collective-permute-start
  14.5 187.3 %sine_convert_fusion = (bf16[10752,1024]{1,0:T(8,128)(2,1)}, bf16[10752,1024]{1,0:T(8,128)(2,1)}) fusion(), kind=kLoop, calls=%fused_computation.8 | loop fusion | flops 121110528 | bytes 44040192 | tf_op jit(solution)/shard_map/convert.19
  201.8 0.7 convert_bitcast_fusion.3
  202.5 29.5 %fusion.9 = bf16[2048,10752]{0,1:T(8,128)(2,1)} fusion(bf16[10752,1024]{1,0:T(8,128)(2,1)} %get-tuple-element.48, bf16[10752,1024]{1,0:T(8,128)(2,1)} %get-tuple-element.49), kind=kLoop, calls=%fused_computation.14 | loop fusion | flops 88080384 | bytes 88080384 | tf_op jit(solution)/shard_map/dot_general | solution.py:36
  232.1 0.1 slice.208
  232.2 0.1 slice.206
  232.4 0.1 slice.158
  232.9 2.4 broadcast_multiply_fusion.1
  235.3 6.7 %collective-permute-start.3 = (bf16[1,10752]{1,0:T(2,128)(2,1)S(1)}, bf16[1,10752]{1,0:T(2,128)(2,1)S(1)}, u32[]{:S(2)}, u32[]{:S(2)}) collective-permute-start(bf16[1,10752]{1,0:T(2,128)(2,1)S(1)} %slice.279), channel_id=1, source_target_pairs={{0,4},{4,8},{8,12},{12,16},{16,20},{20,24},{24,28},{1,5},{5,9},{9,... | collective-permute-start | bytes 64520 | tf_op jit(solution)/shard_map/ppermute | solution.py:18
  242.1 56.8 %copy.41 = bf16[2048,10752]{1,0:T(8,128)(2,1)} copy(bf16[2048,10752]{0,1:T(8,128)(2,1)} %fusion.9) | data formatting | bytes 88080384 | tf_op jit(solution)/shard_map/dot_general | solution.py:36
  299.0 0.9 convert_bitcast_fusion.2
  299.9 19.5 %fusion.66 = bf16[2,1024,2,8]{1,3,2,0:T(8,128)(2,1)S(1)} fusion(bf16[2,1024,10752,1]{2,1,3,0:T(8,128)(2,1)} %bitcast.190, bf16[1,8,10752]{2,1,0:T(8,128)(2,1)S(1)} %get-tuple-element.22, bf16[1,8,10752]{2,1,0:T(8,128)(2,1)S(1)} %copy-done.10, f32[2,8]{1,0:T(2,128)S(1)} %get-tuple-element.46), kind=kOutput, calls=%fused_computation.37 | convolution fusion | flops 705396736 | bytes 44449856 | tf_op jit(solution)/shard_map/dot_general | solution.py:36
  319.3 0.7 copy.42
  320.1 1.1 reshape.79
  321.2 14.8 %all_to_all.72 = bf16[8,2,2048]{2,1,0:T(2,128)(2,1)S(1)} all-to-all(bf16[8,2,2048]{2,1,0:T(2,128)(2,1)S(1)} %reshape.79), channel_id=1, replica_groups=mesh['lat'=8,'deg'=4] {'lat'}, dimensions={0} | all-to-all | bytes 131072 | tf_op jit(solution)/shard_map/all_to_all | solution.py:110
  336.0 1.2 reshape.80
  337.2 1.3 copy.59
  338.6 6.0 %fusion.61 = bf16[2,128,2,64]{3,2,0,1:T(2,128)(2,1)} fusion(bf16[128,64,256]{2,1,0:T(8,128)(2,1)} %param.16, bf16[2,128,2,64]{3,2,0,1:T(2,128)(2,1)S(1)} %copy.45, f32[256]{0:T(256)S(1)} %copy-done.11), kind=kOutput, calls=%fused_computation.34 | convolution fusion | flops 33849344 | bytes 4326400 | tf_op jit(solution)/shard_map/cmfl,mil->cmfi/dot_general | solution.py:46
  344.7 29.1 %all-reduce.5.cloned.1.call-done = bf16[2,128,2,64]{3,2,0,1:T(2,128)(2,1)} async-done(((bf16[2,128,2,64]{3,2,0,1:T(2,128)(2,1)}), bf16[2,128,2,64]{3,2,0,1:T(2,128)(2,1)}) %all-reduce.5.cloned.1.call-update) | async-done | bytes 65552 | tf_op jit(solution)/shard_map/psum | solution.py:112
  373.8 1.7 copy.46
  375.5 5.5 all-to-all-start.1
  381.1 6.8 %all-to-all-done.1 = bf16[2,128,2,64]{1,2,0,3:T(2,128)(2,1)S(1)} async-done(((bf16[2,128,2,64]{1,2,0,3:T(2,128)(2,1)}), bf16[2,128,2,64]{1,2,0,3:T(2,128)(2,1)S(1)}, u32[]{:S(2)}, u32[]{:S(2)}) %all-to-all-start.1) | async-done | bytes 65568 | tf_op jit(solution)/shard_map/all_to_all | solution.py:113
  388.0 18.4 %fusion.10 = f32[2,8,10752]{2,1,0:T(8,128)} fusion(bf16[10752,1024]{1,0:T(8,128)(2,1)} %get-tuple-element.48, bf16[10752,1024]{1,0:T(8,128)(2,1)} %get-tuple-element.49, f32[2,8]{1,0:T(2,128)S(1)} %get-tuple-element.47, bf16[2048,16]{0,1:T(8,128)(2,1)S(1)} %all_to_all.59, bf16[2048]{0:T(1024)(128)(2,1)S(1)} %bitcast.210), kind=kOutput, calls=%fused_computation.15 | convolution fusion | flops 792928256 | bytes 44798016 | tf_op jit(solution)/shard_map/dot_general | solution.py:53
  406.4 1.4 multiply_multiply_fusion
  407.8 1.3 collective-permute-start.4
  409.2 1.3 collective-permute-start.6
  410.5 0.1 slice.220
  410.7 3.0 collective-permute-done.4
  413.8 1.9 collective-permute-done.6
  415.8 2.4 fusion.139
  418.2 4.8 collective-permute-start.5
  423.2 2.3 collective-permute-start.7
  425.5 0.3 convert_bitcast_fusion.1
  425.8 0.1 slice.229
  425.9 1.8 multiply_bitcast_fusion.1
  428.0 0.2 convert_bitcast_fusion
  428.2 19.5 %fusion.67 = bf16[2,1024,2,8]{1,3,2,0:T(8,128)(2,1)S(1)} fusion(bf16[2,1024,10752,1]{2,1,3,0:T(8,128)(2,1)} %bitcast.191, bf16[1,8,10752]{2,1,0:T(8,128)(2,1)S(1)} %get-tuple-element.14, bf16[1,8,10752]{2,1,0:T(8,128)(2,1)S(1)} %get-tuple-element.12, f32[2,8]{1,0:T(2,128)S(1)} %get-tuple-element.46), kind=kOutput, calls=%fused_computation.38 | convolution fusion | flops 705396736 | bytes 44449856 | tf_op jit(solution)/shard_map/dot_general | solution.py:36
  447.7 0.7 copy.49
  448.4 1.1 reshape.81
  449.5 10.5 %all_to_all.73 = bf16[8,2,2048]{2,1,0:T(2,128)(2,1)S(1)} all-to-all(bf16[8,2,2048]{2,1,0:T(2,128)(2,1)S(1)} %reshape.81), channel_id=1, replica_groups=mesh['lat'=8,'deg'=4] {'lat'}, dimensions={0} | all-to-all | bytes 131072 | tf_op jit(solution)/shard_map/all_to_all | solution.py:110
  460.0 1.2 reshape.82
  461.2 1.3 copy.61
  462.5 0.8 copy.52
  463.3 6.1 %fusion.56 = bf16[2,128,2,64]{3,2,0,1:T(2,128)(2,1)} fusion(bf16[128,64,256]{2,1,0:T(8,128)(2,1)} %param.16, bf16[2,128,2,64]{3,2,0,1:T(2,128)(2,1)} %copy.52, f32[256]{0:T(256)S(1)} %copy-done.11), kind=kOutput, calls=%fused_computation.33 | convolution fusion | flops 33849344 | bytes 4326400 | tf_op jit(solution)/shard_map/cmfl,mil->cmfi/dot_general | solution.py:46
  469.4 28.1 %all-reduce.7.cloned.1.call-done = bf16[2,128,2,64]{3,2,0,1:T(2,128)(2,1)} async-done(((bf16[2,128,2,64]{3,2,0,1:T(2,128)(2,1)}), bf16[2,128,2,64]{3,2,0,1:T(2,128)(2,1)}) %all-reduce.7.cloned.1.call-update) | async-done | bytes 65552 | tf_op jit(solution)/shard_map/psum | solution.py:112
  497.6 1.0 copy.53
  498.6 12.2 %all_to_all.74 = bf16[2,128,2,64]{1,2,0,3:T(2,128)(2,1)S(1)} all-to-all(bf16[2,128,2,64]{1,2,0,3:T(2,128)(2,1)S(1)} %copy.53), channel_id=1, replica_groups=mesh['lat'=8,'deg'=4] {'lat'}, dimensions={3} | all-to-all | bytes 131072 | tf_op jit(solution)/shard_map/all_to_all | solution.py:113
  510.9 0.7 all_to_all.67
  511.5 18.4 %fusion.13 = f32[2,8,10752]{2,1,0:T(8,128)} fusion(bf16[10752,1024]{1,0:T(8,128)(2,1)} %get-tuple-element.48, bf16[10752,1024]{1,0:T(8,128)(2,1)} %get-tuple-element.49, f32[2,8]{1,0:T(2,128)S(1)} %get-tuple-element.47, bf16[2048,16]{0,1:T(8,128)(2,1)} %all_to_all.67, bf16[2048]{0:T(1024)(128)(2,1)S(1)} %bitcast.211), kind=kOutput, calls=%fused_computation.16 | convolution fusion | flops 792928256 | bytes 44798016 | tf_op jit(solution)/shard_map/dot_general | solution.py:53
  529.9 1.9 fusion.68
  531.9 1.3 collective-permute-start.8
  533.2 1.9 pad_maximum_fusion.4
  535.1 0.1 slice.238
  535.2 2.5 collective-permute-done.8
  537.8 1.4 fusion.130
  539.3 3.2 collective-permute-start.9
  542.5 0.9 pad_maximum_fusion.3
  543.4 0.7 collective-permute-done.9
  544.2 0.9 fusion.111
  (83 shorter events, 1.8 us)
Async XLA Ops:
  7.2 194.6 %copy-start.2 = (f32[8,10752]{1,0:T(8,128)S(1)}, f32[8,10752]{1,0:T(8,128)}, u32[]{:S(2)}) copy-start(f32[8,10752]{1,0:T(8,128)} %param.9) | copy-start | bytes 1032196
  7.2 366.7 %all-reduce.5.cloned.1.call-start = ((), (), s32[]{:S(2)}) async-start(), calls=%async_computation.4 | async-start | bytes 262144 | tf_op jit(solution)/shard_map/psum | solution.py:112
  8.5 224.2 %collective-permute-start.2 = (bf16[1,10752]{1,0:T(2,128)(2,1)S(1)}, bf16[1,10752]{1,0:T(2,128)(2,1)S(1)}, u32[]{:S(2)}, u32[]{:S(2)}) collective-permute-start(bf16[1,10752]{1,0:T(2,128)(2,1)S(1)} %slice.280), channel_id=1, source_target_pairs={{4,0},{8,4},{12,8},{16,12},{20,16},{24,20},{28,24},{5,1},{9,5},{13... | collective-permute-start | bytes 64520 | tf_op jit(solution)/shard_map/ppermute | solution.py:18
  10.8 221.9 %collective-permute-start.1 = (bf16[1,10752]{1,0:T(2,128)(2,1)S(1)}, bf16[1,10752]{1,0:T(2,128)(2,1)S(1)}, u32[]{:S(2)}, u32[]{:S(2)}) collective-permute-start(bf16[1,10752]{1,0:T(2,128)(2,1)S(1)} %slice.281), channel_id=1, source_target_pairs={{4,0},{8,4},{12,8},{16,12},{20,16},{24,20},{28,24},{5,1},{9,5},{13... | collective-permute-start | bytes 64520 | tf_op jit(solution)/shard_map/ppermute | solution.py:18
  13.2 219.7 %collective-permute-start = (bf16[1,10752]{1,0:T(2,128)(2,1)S(1)}, bf16[1,10752]{1,0:T(2,128)(2,1)S(1)}, u32[]{:S(2)}, u32[]{:S(2)}) collective-permute-start(bf16[1,10752]{1,0:T(2,128)(2,1)S(1)} %slice.282), channel_id=1, source_target_pairs={{4,0},{8,4},{12,8},{16,12},{20,16},{24,20},{28,24},{5,1},{9,5},{13... | collective-permute-start | bytes 64520 | tf_op jit(solution)/shard_map/ppermute | solution.py:18
  202.5 29.9 %copy-start.1 = (f32[8,10752]{1,0:T(8,128)S(1)}, f32[8,10752]{1,0:T(8,128)}, u32[]{:S(2)}) copy-start(f32[8,10752]{1,0:T(8,128)} %param.13) | copy-start | bytes 1032196
  202.5 30.4 %copy-start = (s32[8,10752]{1,0:T(8,128)S(1)}, s32[8,10752]{1,0:T(8,128)}, u32[]{:S(2)}) copy-start(s32[8,10752]{1,0:T(8,128)} %param.15) | copy-start | bytes 1032196
  202.5 30.4 %slice-start = ((f32[8,10752]{1,0:T(8,128)}), f32[8,1]{1,0:T(8,128)S(1)}, s32[]{:S(2)}) async-start(f32[8,10752]{1,0:T(8,128)} %param.13), calls=%async_computation.6 | async-start | bytes 8192 | tf_op jit(solution)/shard_map/jit(_roll_static)/slice | solution.py:87
  235.2 180.5 %copy-start.5 = (f32[8,10752]{1,0:T(8,128)}, f32[8,10752]{1,0:T(8,128)S(1)}, u32[]{:S(2)}) copy-start(f32[8,10752]{1,0:T(8,128)S(1)} %get-tuple-element.34) | copy-start | bytes 1032196
  235.3 63.6 %collective-permute-start.3 = (bf16[1,10752]{1,0:T(2,128)(2,1)S(1)}, bf16[1,10752]{1,0:T(2,128)(2,1)S(1)}, u32[]{:S(2)}, u32[]{:S(2)}) collective-permute-start(bf16[1,10752]{1,0:T(2,128)(2,1)S(1)} %slice.279), channel_id=1, source_target_pairs={{0,4},{4,8},{8,12},{12,16},{16,20},{20,24},{24,28},{1,5},{5,9},{9,... | collective-permute-start | bytes 64520 | tf_op jit(solution)/shard_map/ppermute | solution.py:18
  242.0 57.8 %copy-start.10 = (bf16[1,8,10752]{2,1,0:T(8,128)(2,1)S(1)}, bf16[1,8,10752]{2,1,0:T(8,128)(2,1)}, u32[]{:S(2)}) copy-start(bf16[1,8,10752]{2,1,0:T(8,128)(2,1)} %convert_bitcast_fusion.3) | copy-start | bytes 516100
  298.8 39.8 %copy-start.11 = (f32[256]{0:T(256)S(1)}, f32[256]{0:T(256)}, u32[]{:S(2)}) copy-start(f32[256]{0:T(256)} %param.17) | copy-start | bytes 3076
  338.6 77.2 %copy-start.3 = (f32[8,10752]{1,0:T(8,128)S(1)}, f32[8,10752]{1,0:T(8,128)}, u32[]{:S(2)}) copy-start(f32[8,10752]{1,0:T(8,128)} %param.14) | copy-start | bytes 1032196
  338.6 77.2 %copy-start.7 = (f32[8,10752]{1,0:T(8,128)S(1)}, f32[8,10752]{1,0:T(8,128)}, u32[]{:S(2)}) copy-start(f32[8,10752]{1,0:T(8,128)} %get-tuple-element.35) | copy-start | bytes 1032196
  375.5 12.4 %all-to-all-start.1 = ((bf16[2,128,2,64]{1,2,0,3:T(2,128)(2,1)}), bf16[2,128,2,64]{1,2,0,3:T(2,128)(2,1)S(1)}, u32[]{:S(2)}, u32[]{:S(2)}) async-start(bf16[2,128,2,64]{1,2,0,3:T(2,128)(2,1)} %copy.46), calls=%async_computation.1 | async-start | bytes 131072 | tf_op jit(solution)/shard_map/all_to_all | solution.py:113
  381.0 116.6 %all-reduce.7.cloned.1.call-start = ((), (), s32[]{:S(2)}) async-start(), calls=%async_computation.5 | async-start | bytes 262144 | tf_op jit(solution)/shard_map/psum | solution.py:112
  407.8 5.9 %collective-permute-start.4 = (bf16[1,10752]{1,0:T(2,128)(2,1)S(1)}, bf16[1,10752]{1,0:T(2,128)(2,1)S(1)}, u32[]{:S(2)}, u32[]{:S(2)}) collective-permute-start(bf16[1,10752]{1,0:T(2,128)(2,1)S(1)} %slice.278), channel_id=1, source_target_pairs={{4,0},{8,4},{12,8},{16,12},{20,16},{24,20},{28,24},{5,1},{9,5},{13... | collective-permute-start | bytes 64520 | tf_op jit(solution)/shard_map/ppermute | solution.py:18
  409.2 6.5 %collective-permute-start.6 = (bf16[1,10752]{1,0:T(2,128)(2,1)S(1)}, bf16[1,10752]{1,0:T(2,128)(2,1)S(1)}, u32[]{:S(2)}, u32[]{:S(2)}) collective-permute-start(bf16[1,10752]{1,0:T(2,128)(2,1)S(1)} %slice.276), channel_id=1, source_target_pairs={{4,0},{8,4},{12,8},{16,12},{20,16},{24,20},{28,24},{5,1},{9,5},{13... | collective-permute-start | bytes 64520 | tf_op jit(solution)/shard_map/ppermute | solution.py:18
  418.2 7.3 %collective-permute-start.5 = (bf16[1,10752]{1,0:T(2,128)(2,1)S(1)}, bf16[1,10752]{1,0:T(2,128)(2,1)S(1)}, u32[]{:S(2)}, u32[]{:S(2)}) collective-permute-start(bf16[1,10752]{1,0:T(2,128)(2,1)S(1)} %slice.277), channel_id=1, source_target_pairs={{0,4},{4,8},{8,12},{12,16},{16,20},{20,24},{24,28},{1,5},{5,9},{9,... | collective-permute-start | bytes 64520 | tf_op jit(solution)/shard_map/ppermute | solution.py:18
  423.2 4.8 collective-permute-start.7
  460.0 73.2 %copy-start.9 = (f32[1,8,10752]{2,1,0:T(8,128)S(1)}, f32[1,8,10752]{2,1,0:T(8,128)}, u32[]{:S(2)}) copy-start(f32[1,8,10752]{2,1,0:T(8,128)} %get-tuple-element.4) | copy-start | bytes 1032196
  463.3 74.5 %copy-start.4 = (f32[8,10752]{1,0:T(8,128)S(1)}, f32[8,10752]{1,0:T(8,128)}, u32[]{:S(2)}) copy-start(f32[8,10752]{1,0:T(8,128)} %param.14) | copy-start | bytes 1032196
  463.3 74.5 %copy-start.6 = (f32[8,10752]{1,0:T(8,128)S(1)}, f32[8,10752]{1,0:T(8,128)}, u32[]{:S(2)}) copy-start(f32[8,10752]{1,0:T(8,128)} %copy-done.5) | copy-start | bytes 1032196
  463.3 74.5 %copy-start.8 = (f32[8,10752]{1,0:T(8,128)S(1)}, f32[8,10752]{1,0:T(8,128)}, u32[]{:S(2)}) copy-start(f32[8,10752]{1,0:T(8,128)} %get-tuple-element.35) | copy-start | bytes 1032196
  531.9 5.9 %collective-permute-start.8 = (bf16[1,10752]{1,0:T(2,128)(2,1)S(1)}, bf16[1,10752]{1,0:T(2,128)(2,1)S(1)}, u32[]{:S(2)}, u32[]{:S(2)}) collective-permute-start(bf16[1,10752]{1,0:T(2,128)(2,1)S(1)} %slice.274), channel_id=1, source_target_pairs={{4,0},{8,4},{12,8},{16,12},{20,16},{24,20},{28,24},{5,1},{9,5},{13... | collective-permute-start | bytes 64520 | tf_op jit(solution)/shard_map/ppermute | solution.py:18
  539.3 4.9 collective-permute-start.9
Sparse Core Ops, SparseCore 0:
  344.8 28.9 all-reduce.4
  469.6 27.9 all-reduce.6
where the time goes:
time: 554 us; the launch traced here: 552 us
  other arithmetic  237 us (43%)
  matrix products  88 us (16%)
  local copies, waits for them, and re-layouts  72.5 us (13%)
  waiting for transfers between devices  72.3 us (13%)
  blocking collectives  37.5 us (7%)
  starting transfers between devices  30.4 us (5%)
  between operations  14.7 us (3%)
    another operation x1, other arithmetic  187 us
    psum x2, waiting for transfers between devices, on_device(): total_sum = lax.psum(partial_value.astype(jnp.bfloat16), 'deg')  57.2 us
    dot_general x1, local copies, waits for them, and re-layouts, analyse(): lax.dot_general(table_now, flat_rows, (((0,), (1,)), ((), ())), preferred...  56.8 us
    dot_general x2, matrix products, analyse(): lax.dot_general(table_now, flat_rows, (((0,), (1,)), ((), ())), preferred...  39 us
    dot_general x2, matrix products, synthesise(): lax.dot_general(scaled, table_now, (((0,), (1,)), ((), ())), preferred_el...  36.8 us
    dot_general x1, other arithmetic, analyse(): lax.dot_general(table_now, flat_rows, (((0,), (1,)), ((), ())), preferred...  29.5 us
    all_to_all x2, blocking collectives, on_device(): lax.all_to_all(spectra, 'lat', split_axis=1, concat_axis=3, tiled=True)  25.3 us
    ppermute x10, starting transfers between devices, passed_along(): return lax.ppermute(value, axis, pairs)  24.8 us
  transfers between devices with their start and end apart: 13, of which 7 were waited for; matrix products, arithmetic and copies ran while one was open for 51% of the time, Pallas kernels for 0%

commit v1 on v0

--- a/solution.py
+++ b/solution.py
@@ -110,7 +110,22 @@
         owned_rows = lax.all_to_all(spectra, "lat", split_axis=1, concat_axis=3, tiled=True)
         partial_value = legendre(owned_rows, basis, love)
         total_sum = lax.psum(partial_value.astype(jnp.bfloat16), "deg")
-        banded = lax.all_to_all(total_sum, "lat", split_axis=3, concat_axis=1, tiled=True)
+        outcome_arr, f_next = (lax.axis_size("lat"), lax.axis_index("lat"))
+        o_now = total_sum.shape[3] // outcome_arr
+        v_next = list(total_sum.shape)
+        v_next[3] = o_now
+        far_arr = v_next[1]
+        v_next[1] = far_arr * outcome_arr
+        banded = jnp.zeros(v_next, total_sum.dtype)
+        for src_i in range(outcome_arr):
+            d_next = lax.dynamic_slice_in_dim(total_sum, (f_next ^ src_i) * o_now, o_now, axis=3)
+            if src_i:
+                d_next = lax.ppermute(
+                    d_next, "lat", tuple(((t, t ^ src_i) for t in range(outcome_arr)))
+                )
+            banded = lax.dynamic_update_slice_in_dim(
+                banded, d_next, (f_next ^ src_i) * far_arr, axis=1
+            )
         loads = synthesise(banded, full_factor, full_table, output_weight)
         psi_now = state_eta - loads[0]
         psi_up = jnp.concatenate([psi_now[1:], from_north(psi_now[:1])], 0)

time: 554 us -> 591 us (1.067)
  starting transfers between devices: 30.4 us -> 47.7 us
  local copies, waits for them, and re-layouts: 72.5 us -> 87.3 us
  waiting for transfers between devices: 72.3 us -> 85.8 us
  blocking collectives: 37.5 us -> 27.4 us
    ppermute x0 -> x14, starting transfers between devices: none -> 22.5 us  [on_device(): lax.ppermute(d_next, 'lat', tuple(((t, t ^ src_i) for t in range(outcome_...]
    ppermute x0 -> x14, waiting for transfers between devices: none -> 20.2 us  [on_device(): lax.ppermute(d_next, 'lat', tuple(((t, t ^ src_i) for t in range(outcome_...]
    ppermute x0 -> x14, local copies, waits for them, and re-layouts: none -> 13.9 us  [on_device(): lax.ppermute(d_next, 'lat', tuple(((t, t ^ src_i) for t in range(outcome_...]
    all_to_all x1 -> x0, blocking collectives: 12.2 us -> none  [on_device(): lax.all_to_all(total_sum, 'lat', split_axis=3, concat_axis=1, tiled=True)]
    dynamic_slice x0 -> x4, local copies, waits for them, and re-layouts: none -> 8.45 us  [on_device(): lax.dynamic_slice_in_dim(total_sum, (f_next ^ src_i) * o_now, o_now, axis=3)]
    all_to_all x1 -> x0, waiting for transfers between devices: 6.84 us -> none  [on_device(): lax.all_to_all(total_sum, 'lat', split_axis=3, concat_axis=1, tiled=True)]
  transfers between devices with their start and end apart: 13 -> 26, of which waited for: 7 -> 10; matrix products, arithmetic and copies ran while one was open for 51% -> 49% of each run, Pallas kernels for 0% -> 0%
where the time goes in v1:
time: 591 us; the launch traced here: 588 us
  other arithmetic  237 us (40%)
  matrix products  87.8 us (15%)
  local copies, waits for them, and re-layouts  87.3 us (15%)
  waiting for transfers between devices  85.8 us (15%)
  starting transfers between devices  47.7 us (8%)
  blocking collectives  27.4 us (5%)
  between operations  15 us (3%)
    another operation x1, other arithmetic  187 us
    psum x2, waiting for transfers between devices, on_device(): total_sum = lax.psum(partial_value.astype(jnp.bfloat16), 'deg')  57.4 us
    dot_general x1, local copies, waits for them, and re-layouts, analyse(): lax.dot_general(table_now, flat_rows, (((0,), (1,)), ((), ())), preferred...  51.3 us
    dot_general x2, matrix products, analyse(): lax.dot_general(table_now, flat_rows, (((0,), (1,)), ((), ())), preferred...  38.8 us
    dot_general x2, matrix products, synthesise(): lax.dot_general(scaled, table_now, (((0,), (1,)), ((), ())), preferred_el...  36.8 us
    dot_general x1, other arithmetic, analyse(): lax.dot_general(table_now, flat_rows, (((0,), (1,)), ((), ())), preferred...  29.5 us
    all_to_all x2, blocking collectives, on_device(): lax.all_to_all(spectra, 'lat', split_axis=1, concat_axis=3, tiled=True)  27.4 us
    ppermute x10, starting transfers between devices, passed_along(): return lax.ppermute(value, axis, pairs)  25.1 us
  transfers between devices with their start and end apart: 26, of which 10 were waited for; matrix products, arithmetic and copies ran while one was open for 49% of the time, Pallas kernels for 0%

profile of v1, /device:TPU:0, one launch (start us, length us, event | category | flops | bytes accessed | tf_op | source)
XLA Modules:
  0.0 587.8 jit_solution(3181989039960776486)
XLA Ops:
  7.3 1.2 multiply_multiply_fusion.3
  8.5 1.3 collective-permute-start.2
  9.8 1.0 slice.281
  10.8 1.3 collective-permute-start.1
  12.1 1.0 convert_element_type.110
  13.2 1.3 collective-permute-start
  14.5 187.3 %sine_convert_fusion = (bf16[10752,1024]{1,0:T(8,128)(2,1)}, bf16[10752,1024]{1,0:T(8,128)(2,1)}) fusion(), kind=kLoop, calls=%fused_computation.8 | loop fusion | flops 121110528 | bytes 44040192 | tf_op jit(solution)/shard_map/convert.19
  202.5 29.5 %fusion.9 = bf16[2048,10752]{0,1:T(8,128)(2,1)} fusion(bf16[10752,1024]{1,0:T(8,128)(2,1)} %get-tuple-element.64, bf16[10752,1024]{1,0:T(8,128)(2,1)} %get-tuple-element.65), kind=kLoop, calls=%fused_computation.14 | loop fusion | flops 88080384 | bytes 88080384 | tf_op jit(solution)/shard_map/dot_general | solution.py:36
  232.8 2.4 broadcast_multiply_fusion.1
  235.2 6.7 %collective-permute-start.3 = (bf16[1,10752]{1,0:T(2,128)(2,1)S(1)}, bf16[1,10752]{1,0:T(2,128)(2,1)S(1)}, u32[]{:S(2)}, u32[]{:S(2)}) collective-permute-start(bf16[1,10752]{1,0:T(2,128)(2,1)S(1)} %slice.279), channel_id=1, source_target_pairs={{0,4},{4,8},{8,12},{12,16},{16,20},{20,24},{24,28},{1,5},{5,9},{9,... | collective-permute-start | bytes 64520 | tf_op jit(solution)/shard_map/ppermute | solution.py:18
  242.0 51.3 %copy.73 = bf16[2048,10752]{1,0:T(8,128)(2,1)} copy(bf16[2048,10752]{0,1:T(8,128)(2,1)} %fusion.9) | data formatting | bytes 88080384 | tf_op jit(solution)/shard_map/dot_general | solution.py:36
  294.3 19.4 %fusion.66 = bf16[2,1024,2,8]{1,3,2,0:T(8,128)(2,1)S(1)} fusion(bf16[2,1024,10752,1]{2,1,3,0:T(8,128)(2,1)} %bitcast.179, bf16[1,8,10752]{2,1,0:T(8,128)(2,1)S(1)} %get-tuple-element.22, bf16[1,8,10752]{2,1,0:T(8,128)(2,1)S(1)} %copy-done.10, f32[2,8]{1,0:T(2,128)S(1)} %get-tuple-element.62), kind=kOutput, calls=%fused_computation.37 | convolution fusion | flops 705396736 | bytes 44449856 | tf_op jit(solution)/shard_map/dot_general | solution.py:36
  314.5 1.1 reshape.81
  315.5 14.8 %all_to_all.36 = bf16[8,2,2048]{2,1,0:T(2,128)(2,1)S(1)} all-to-all(bf16[8,2,2048]{2,1,0:T(2,128)(2,1)S(1)} %reshape.81), channel_id=1, replica_groups=mesh['lat'=8,'deg'=4] {'lat'}, dimensions={0} | all-to-all | bytes 131072 | tf_op jit(solution)/shard_map/all_to_all | solution.py:110
  330.3 1.2 reshape.82
  331.5 1.3 copy.101
  333.0 6.0 %fusion.61 = bf16[2,128,2,64]{3,2,0,1:T(2,128)(2,1)} fusion(bf16[128,64,256]{2,1,0:T(8,128)(2,1)} %param.16, bf16[2,128,2,64]{3,2,0,1:T(2,128)(2,1)S(1)} %copy.77, f32[256]{0:T(256)S(1)} %copy-done.12), kind=kOutput, calls=%fused_computation.34 | convolution fusion | flops 33849344 | bytes 4326400 | tf_op jit(solution)/shard_map/cmfl,mil->cmfi/dot_general | solution.py:46
  339.2 29.0 %all-reduce.5.cloned.1.call-done = bf16[2,128,2,64]{3,2,0,1:T(2,128)(2,1)} async-done(((bf16[2,128,2,64]{3,2,0,1:T(2,128)(2,1)}), bf16[2,128,2,64]{3,2,0,1:T(2,128)(2,1)}) %all-reduce.5.cloned.1.call-update) | async-done | bytes 65552 | tf_op jit(solution)/shard_map/psum | solution.py:112
  368.2 3.7 constant_dynamic-slice_fusion.8
  371.9 1.5 collective-permute-start.4
  373.4 1.5 collective-permute-start.5
  375.5 2.4 collective-permute-start.7
  377.9 1.4 collective-permute-start.8
  380.0 3.3 collective-permute-start.9
  386.0 1.0 copy.81
  387.1 6.9 %collective-permute-done.7 = bf16[2,128,2,8]{3,2,0,1:T(2,128)(2,1)} collective-permute-done((bf16[2,128,2,8]{3,2,0,1:T(2,128)(2,1)S(1)}, bf16[2,128,2,8]{3,2,0,1:T(2,128)(2,1)}, u32[]{:S(2)}, u32[]{:S(2)}) %collective-permute-start.7) | collective-permute-done | bytes 8224 | tf_op jit(solution)/shard_map/ppermute | solution.py:123
  395.0 2.8 collective-permute-done.8
  398.9 1.0 copy.84
  399.9 1.0 copy.85
  401.1 18.4 %fusion.10 = f32[2,8,10752]{2,1,0:T(8,128)} fusion(bf16[10752,1024]{1,0:T(8,128)(2,1)} %get-tuple-element.64, bf16[10752,1024]{1,0:T(8,128)(2,1)} %get-tuple-element.65, f32[2,8]{1,0:T(2,128)S(1)} %get-tuple-element.63, bf16[2048,16]{0,1:T(8,128)(2,1)S(1)} %bitcast.198), kind=kOutput, calls=%fused_computation.15 | convolution fusion | flops 792895488 | bytes 44793920 | tf_op jit(solution)/shard_map/dot_general | solution.py:53
  419.5 1.4 multiply_multiply_fusion
  420.9 1.3 collective-permute-start.11
  422.2 1.3 collective-permute-start.13
  423.8 3.0 collective-permute-done.11
  426.9 1.9 collective-permute-done.13
  428.9 2.4 fusion.135
  431.3 4.8 collective-permute-start.12
  436.2 2.6 collective-permute-start.14
  439.3 1.8 multiply_bitcast_fusion.1
  441.6 19.4 %fusion.67 = bf16[2,1024,2,8]{1,3,2,0:T(8,128)(2,1)S(1)} fusion(bf16[2,1024,10752,1]{2,1,3,0:T(8,128)(2,1)} %bitcast.180, bf16[1,8,10752]{2,1,0:T(8,128)(2,1)S(1)} %get-tuple-element.14, bf16[1,8,10752]{2,1,0:T(8,128)(2,1)S(1)} %get-tuple-element.12, f32[2,8]{1,0:T(2,128)S(1)} %get-tuple-element.62), kind=kOutput, calls=%fused_computation.38 | convolution fusion | flops 705396736 | bytes 44449856 | tf_op jit(solution)/shard_map/dot_general | solution.py:36
  461.7 1.1 reshape.83
  462.8 12.6 %all_to_all.37 = bf16[8,2,2048]{2,1,0:T(2,128)(2,1)S(1)} all-to-all(bf16[8,2,2048]{2,1,0:T(2,128)(2,1)S(1)} %reshape.83), channel_id=1, replica_groups=mesh['lat'=8,'deg'=4] {'lat'}, dimensions={0} | all-to-all | bytes 131072 | tf_op jit(solution)/shard_map/all_to_all | solution.py:110
  475.4 1.2 reshape.84
  476.6 1.3 copy.103
  478.7 6.1 %fusion.56 = bf16[2,128,2,64]{3,2,0,1:T(2,128)(2,1)} fusion(bf16[128,64,256]{2,1,0:T(8,128)(2,1)} %param.16, bf16[2,128,2,64]{3,2,0,1:T(2,128)(2,1)} %copy.89, f32[256]{0:T(256)S(1)} %copy-done.12), kind=kOutput, calls=%fused_computation.33 | convolution fusion | flops 33849344 | bytes 4326400 | tf_op jit(solution)/shard_map/cmfl,mil->cmfi/dot_general | solution.py:46
  484.9 28.4 %all-reduce.7.cloned.1.call-done = bf16[2,128,2,64]{3,2,0,1:T(2,128)(2,1)} async-done(((bf16[2,128,2,64]{3,2,0,1:T(2,128)(2,1)}), bf16[2,128,2,64]{3,2,0,1:T(2,128)(2,1)}) %all-reduce.7.cloned.1.call-update) | async-done | bytes 65552 | tf_op jit(solution)/shard_map/psum | solution.py:112
  513.3 3.7 constant_dynamic-slice_fusion
  518.0 1.5 collective-permute-start.15
  519.5 1.5 collective-permute-start.16
  521.6 2.4 collective-permute-start.18
  524.0 1.4 collective-permute-start.19
  525.5 3.4 collective-permute-start.20
  531.5 1.0 copy.93
  532.6 7.6 %collective-permute-done.18 = bf16[2,128,2,8]{3,2,0,1:T(2,128)(2,1)} collective-permute-done((bf16[2,128,2,8]{3,2,0,1:T(2,128)(2,1)}, bf16[2,128,2,8]{3,2,0,1:T(2,128)(2,1)}, u32[]{:S(2)}, u32[]{:S(2)}) %collective-permute-start.18) | collective-permute-done | bytes 8224 | tf_op jit(solution)/shard_map/ppermute | solution.py:123
  541.3 2.9 collective-permute-done.19
  545.2 1.0 copy.96
  546.2 1.0 copy.97
  547.4 18.4 %fusion.13 = f32[2,8,10752]{2,1,0:T(8,128)} fusion(bf16[10752,1024]{1,0:T(8,128)(2,1)} %get-tuple-element.64, bf16[10752,1024]{1,0:T(8,128)(2,1)} %get-tuple-element.65, f32[2,8]{1,0:T(2,128)S(1)} %get-tuple-element.63, bf16[2048,16]{0,1:T(8,128)(2,1)S(1)} %bitcast.197), kind=kOutput, calls=%fused_computation.16 | convolution fusion | flops 792895488 | bytes 44793920 | tf_op jit(solution)/shard_map/dot_general | solution.py:53
  565.8 1.9 fusion.68
  567.7 1.3 collective-permute-start.22
  569.0 1.9 pad_maximum_fusion.4
  571.1 2.5 collective-permute-done.22
  573.7 1.4 fusion.126
  575.1 3.2 collective-permute-start.23
  (140 shorter events, 22.2 us)
Async XLA Ops:
  7.2 194.6 %copy-start.2 = (f32[8,10752]{1,0:T(8,128)S(1)}, f32[8,10752]{1,0:T(8,128)}, u32[]{:S(2)}) copy-start(f32[8,10752]{1,0:T(8,128)} %param.9) | copy-start | bytes 1032196
  7.2 361.0 %all-reduce.5.cloned.1.call-start = ((), (), s32[]{:S(2)}) async-start(), calls=%async_computation.2 | async-start | bytes 262144 | tf_op jit(solution)/shard_map/psum | solution.py:112
  8.5 224.1 %collective-permute-start.2 = (bf16[1,10752]{1,0:T(2,128)(2,1)S(1)}, bf16[1,10752]{1,0:T(2,128)(2,1)S(1)}, u32[]{:S(2)}, u32[]{:S(2)}) collective-permute-start(bf16[1,10752]{1,0:T(2,128)(2,1)S(1)} %slice.280), channel_id=1, source_target_pairs={{4,0},{8,4},{12,8},{16,12},{20,16},{24,20},{28,24},{5,1},{9,5},{13... | collective-permute-start | bytes 64520 | tf_op jit(solution)/shard_map/ppermute | solution.py:18
  10.8 221.9 %collective-permute-start.1 = (bf16[1,10752]{1,0:T(2,128)(2,1)S(1)}, bf16[1,10752]{1,0:T(2,128)(2,1)S(1)}, u32[]{:S(2)}, u32[]{:S(2)}) collective-permute-start(bf16[1,10752]{1,0:T(2,128)(2,1)S(1)} %slice.281), channel_id=1, source_target_pairs={{4,0},{8,4},{12,8},{16,12},{20,16},{24,20},{28,24},{5,1},{9,5},{13... | collective-permute-start | bytes 64520 | tf_op jit(solution)/shard_map/ppermute | solution.py:18
  13.2 219.6 %collective-permute-start = (bf16[1,10752]{1,0:T(2,128)(2,1)S(1)}, bf16[1,10752]{1,0:T(2,128)(2,1)S(1)}, u32[]{:S(2)}, u32[]{:S(2)}) collective-permute-start(bf16[1,10752]{1,0:T(2,128)(2,1)S(1)} %slice.282), channel_id=1, source_target_pairs={{4,0},{8,4},{12,8},{16,12},{20,16},{24,20},{28,24},{5,1},{9,5},{13... | collective-permute-start | bytes 64520 | tf_op jit(solution)/shard_map/ppermute | solution.py:18
  202.5 29.9 %copy-start.1 = (f32[8,10752]{1,0:T(8,128)S(1)}, f32[8,10752]{1,0:T(8,128)}, u32[]{:S(2)}) copy-start(f32[8,10752]{1,0:T(8,128)} %param.13) | copy-start | bytes 1032196
  202.5 30.3 %copy-start = (s32[8,10752]{1,0:T(8,128)S(1)}, s32[8,10752]{1,0:T(8,128)}, u32[]{:S(2)}) copy-start(s32[8,10752]{1,0:T(8,128)} %param.15) | copy-start | bytes 1032196
  202.5 30.3 %slice-start = ((f32[8,10752]{1,0:T(8,128)}), f32[8,1]{1,0:T(8,128)S(1)}, s32[]{:S(2)}) async-start(f32[8,10752]{1,0:T(8,128)} %param.13), calls=%async_computation.4 | async-start | bytes 8192 | tf_op jit(solution)/shard_map/jit(_roll_static)/slice | solution.py:87
  235.2 193.6 %copy-start.5 = (f32[8,10752]{1,0:T(8,128)}, f32[8,10752]{1,0:T(8,128)S(1)}, u32[]{:S(2)}) copy-start(f32[8,10752]{1,0:T(8,128)S(1)} %get-tuple-element.34) | copy-start | bytes 1032196
  235.2 58.1 %collective-permute-start.3 = (bf16[1,10752]{1,0:T(2,128)(2,1)S(1)}, bf16[1,10752]{1,0:T(2,128)(2,1)S(1)}, u32[]{:S(2)}, u32[]{:S(2)}) collective-permute-start(bf16[1,10752]{1,0:T(2,128)(2,1)S(1)} %slice.279), channel_id=1, source_target_pairs={{0,4},{4,8},{8,12},{12,16},{16,20},{20,24},{24,28},{1,5},{5,9},{9,... | collective-permute-start | bytes 64520 | tf_op jit(solution)/shard_map/ppermute | solution.py:18
  242.0 52.3 %copy-start.10 = (bf16[1,8,10752]{2,1,0:T(8,128)(2,1)S(1)}, bf16[1,8,10752]{2,1,0:T(8,128)(2,1)}, u32[]{:S(2)}) copy-start(bf16[1,8,10752]{2,1,0:T(8,128)(2,1)} %convert_bitcast_fusion.3) | copy-start | bytes 516100
  293.3 39.7 %copy-start.12 = (f32[256]{0:T(256)S(1)}, f32[256]{0:T(256)}, u32[]{:S(2)}) copy-start(f32[256]{0:T(256)} %param.17) | copy-start | bytes 3076
  333.0 95.9 %copy-start.3 = (f32[8,10752]{1,0:T(8,128)S(1)}, f32[8,10752]{1,0:T(8,128)}, u32[]{:S(2)}) copy-start(f32[8,10752]{1,0:T(8,128)} %param.14) | copy-start | bytes 1032196
  333.0 95.9 %copy-start.7 = (f32[8,10752]{1,0:T(8,128)S(1)}, f32[8,10752]{1,0:T(8,128)}, u32[]{:S(2)}) copy-start(f32[8,10752]{1,0:T(8,128)} %get-tuple-element.35) | copy-start | bytes 1032196
  339.1 174.2 %all-reduce.7.cloned.1.call-start = ((), (), s32[]{:S(2)}) async-start(), calls=%async_computation.3 | async-start | bytes 262144 | tf_op jit(solution)/shard_map/psum | solution.py:112
  371.9 7.4 %collective-permute-start.4 = (bf16[2,128,2,8]{3,2,0,1:T(2,128)(2,1)}, bf16[2,128,2,8]{3,2,0,1:T(2,128)(2,1)S(1)}, u32[]{:S(2)}, u32[]{:S(2)}) collective-permute-start(bf16[2,128,2,8]{3,2,0,1:T(2,128)(2,1)} %get-tuple-element.60), channel_id=1, source_target_pairs={{0,4},{4,0},{8,12},{12,8},{16,20},{20,16},{24,28},{28,24},{1,5},{5... | collective-permute-start | bytes 24584 | tf_op jit(solution)/shard_map/ppermute | solution.py:123
  373.4 11.0 %collective-permute-start.5 = (bf16[2,128,2,8]{3,2,0,1:T(2,128)(2,1)}, bf16[2,128,2,8]{3,2,0,1:T(2,128)(2,1)}, u32[]{:S(2)}, u32[]{:S(2)}) collective-permute-start(bf16[2,128,2,8]{3,2,0,1:T(2,128)(2,1)} %get-tuple-element.59), channel_id=1, source_target_pairs={{0,8},{4,12},{8,0},{12,4},{16,24},{20,28},{24,16},{28,20},{1,9},{5... | collective-permute-start | bytes 24584 | tf_op jit(solution)/shard_map/ppermute | solution.py:123
  374.9 11.1 %collective-permute-start.6 = (bf16[2,128,2,8]{3,2,0,1:T(2,128)(2,1)}, bf16[2,128,2,8]{3,2,0,1:T(2,128)(2,1)}, u32[]{:S(2)}, u32[]{:S(2)}) collective-permute-start(bf16[2,128,2,8]{3,2,0,1:T(2,128)(2,1)} %get-tuple-element.58), channel_id=1, source_target_pairs={{0,12},{4,8},{8,4},{12,0},{16,28},{20,24},{24,20},{28,16},{1,13},{... | collective-permute-start | bytes 24584 | tf_op jit(solution)/shard_map/ppermute | solution.py:123
  375.5 18.5 %collective-permute-start.7 = (bf16[2,128,2,8]{3,2,0,1:T(2,128)(2,1)S(1)}, bf16[2,128,2,8]{3,2,0,1:T(2,128)(2,1)}, u32[]{:S(2)}, u32[]{:S(2)}) collective-permute-start(bf16[2,128,2,8]{3,2,0,1:T(2,128)(2,1)S(1)} %get-tuple-element.57), channel_id=1, source_target_pairs={{0,16},{4,20},{8,24},{12,28},{16,0},{20,4},{24,8},{28,12},{1,17},{... | collective-permute-start | bytes 24584 | tf_op jit(solution)/shard_map/ppermute | solution.py:123
  377.9 19.9 %collective-permute-start.8 = (bf16[2,128,2,8]{3,2,0,1:T(2,128)(2,1)S(1)}, bf16[2,128,2,8]{3,2,0,1:T(2,128)(2,1)}, u32[]{:S(2)}, u32[]{:S(2)}) collective-permute-start(bf16[2,128,2,8]{3,2,0,1:T(2,128)(2,1)S(1)} %get-tuple-element.56), channel_id=1, source_target_pairs={{0,20},{4,16},{8,28},{12,24},{16,4},{20,0},{24,12},{28,8},{1,21},{... | collective-permute-start | bytes 24584 | tf_op jit(solution)/shard_map/ppermute | solution.py:123
  379.4 0.7 copy-start.11
  380.0 18.8 %collective-permute-start.9 = (bf16[2,128,2,8]{3,2,0,1:T(2,128)(2,1)S(1)}, bf16[2,128,2,8]{3,2,0,1:T(2,128)(2,1)}, u32[]{:S(2)}, u32[]{:S(2)}) collective-permute-start(bf16[2,128,2,8]{3,2,0,1:T(2,128)(2,1)S(1)} %get-tuple-element.55), channel_id=1, source_target_pairs={{0,24},{4,28},{8,16},{12,20},{16,8},{20,12},{24,0},{28,4},{1,25},{... | collective-permute-start | bytes 24584 | tf_op jit(solution)/shard_map/ppermute | solution.py:123
  384.4 15.5 %collective-permute-start.10 = (bf16[2,128,2,8]{3,2,0,1:T(2,128)(2,1)S(1)}, bf16[2,128,2,8]{3,2,0,1:T(2,128)(2,1)}, u32[]{:S(2)}, u32[]{:S(2)}) collective-permute-start(bf16[2,128,2,8]{3,2,0,1:T(2,128)(2,1)S(1)} %get-tuple-element.54), channel_id=1, source_target_pairs={{0,28},{4,24},{8,20},{12,16},{16,12},{20,8},{24,4},{28,0},{1,29},{... | collective-permute-start | bytes 24584 | tf_op jit(solution)/shard_map/ppermute | solution.py:123
  420.9 5.9 %collective-permute-start.11 = (bf16[1,10752]{1,0:T(2,128)(2,1)S(1)}, bf16[1,10752]{1,0:T(2,128)(2,1)S(1)}, u32[]{:S(2)}, u32[]{:S(2)}) collective-permute-start(bf16[1,10752]{1,0:T(2,128)(2,1)S(1)} %slice.278), channel_id=1, source_target_pairs={{4,0},{8,4},{12,8},{16,12},{20,16},{24,20},{28,24},{5,1},{9,5},{13... | collective-permute-start | bytes 64520 | tf_op jit(solution)/shard_map/ppermute | solution.py:18
  422.2 6.5 %collective-permute-start.13 = (bf16[1,10752]{1,0:T(2,128)(2,1)S(1)}, bf16[1,10752]{1,0:T(2,128)(2,1)S(1)}, u32[]{:S(2)}, u32[]{:S(2)}) collective-permute-start(bf16[1,10752]{1,0:T(2,128)(2,1)S(1)} %slice.276), channel_id=1, source_target_pairs={{4,0},{8,4},{12,8},{16,12},{20,16},{24,20},{28,24},{5,1},{9,5},{13... | collective-permute-start | bytes 64520 | tf_op jit(solution)/shard_map/ppermute | solution.py:18
  431.3 7.5 %collective-permute-start.12 = (bf16[1,10752]{1,0:T(2,128)(2,1)S(1)}, bf16[1,10752]{1,0:T(2,128)(2,1)S(1)}, u32[]{:S(2)}, u32[]{:S(2)}) collective-permute-start(bf16[1,10752]{1,0:T(2,128)(2,1)S(1)} %slice.277), channel_id=1, source_target_pairs={{0,4},{4,8},{8,12},{12,16},{16,20},{20,24},{24,28},{1,5},{5,9},{9,... | collective-permute-start | bytes 64520 | tf_op jit(solution)/shard_map/ppermute | solution.py:18
  436.2 5.1 collective-permute-start.14
  478.7 90.3 %copy-start.9 = (f32[1,8,10752]{2,1,0:T(8,128)S(1)}, f32[1,8,10752]{2,1,0:T(8,128)}, u32[]{:S(2)}) copy-start(f32[1,8,10752]{2,1,0:T(8,128)} %get-tuple-element.4) | copy-start | bytes 1032196
  478.7 95.0 %copy-start.4 = (f32[8,10752]{1,0:T(8,128)S(1)}, f32[8,10752]{1,0:T(8,128)}, u32[]{:S(2)}) copy-start(f32[8,10752]{1,0:T(8,128)} %param.14) | copy-start | bytes 1032196
  478.7 95.0 %copy-start.6 = (f32[8,10752]{1,0:T(8,128)S(1)}, f32[8,10752]{1,0:T(8,128)}, u32[]{:S(2)}) copy-start(f32[8,10752]{1,0:T(8,128)} %copy-done.5) | copy-start | bytes 1032196
  478.7 95.0 %copy-start.8 = (f32[8,10752]{1,0:T(8,128)S(1)}, f32[8,10752]{1,0:T(8,128)}, u32[]{:S(2)}) copy-start(f32[8,10752]{1,0:T(8,128)} %get-tuple-element.35) | copy-start | bytes 1032196
  518.0 7.4 %collective-permute-start.15 = (bf16[2,128,2,8]{3,2,0,1:T(2,128)(2,1)}, bf16[2,128,2,8]{3,2,0,1:T(2,128)(2,1)}, u32[]{:S(2)}, u32[]{:S(2)}) collective-permute-start(bf16[2,128,2,8]{3,2,0,1:T(2,128)(2,1)} %get-tuple-element.52), channel_id=1, source_target_pairs={{0,4},{4,0},{8,12},{12,8},{16,20},{20,16},{24,28},{28,24},{1,5},{5... | collective-permute-start | bytes 24584 | tf_op jit(solution)/shard_map/ppermute | solution.py:123
  519.5 10.4 %collective-permute-start.16 = (bf16[2,128,2,8]{3,2,0,1:T(2,128)(2,1)}, bf16[2,128,2,8]{3,2,0,1:T(2,128)(2,1)}, u32[]{:S(2)}, u32[]{:S(2)}) collective-permute-start(bf16[2,128,2,8]{3,2,0,1:T(2,128)(2,1)} %get-tuple-element.51), channel_id=1, source_target_pairs={{0,8},{4,12},{8,0},{12,4},{16,24},{20,28},{24,16},{28,20},{1,9},{5... | collective-permute-start | bytes 24584 | tf_op jit(solution)/shard_map/ppermute | solution.py:123
  521.0 10.5 %collective-permute-start.17 = (bf16[2,128,2,8]{3,2,0,1:T(2,128)(2,1)}, bf16[2,128,2,8]{3,2,0,1:T(2,128)(2,1)}, u32[]{:S(2)}, u32[]{:S(2)}) collective-permute-start(bf16[2,128,2,8]{3,2,0,1:T(2,128)(2,1)} %get-tuple-element.50), channel_id=1, source_target_pairs={{0,12},{4,8},{8,4},{12,0},{16,28},{20,24},{24,20},{28,16},{1,13},{... | collective-permute-start | bytes 24584 | tf_op jit(solution)/shard_map/ppermute | solution.py:123
  521.6 18.6 %collective-permute-start.18 = (bf16[2,128,2,8]{3,2,0,1:T(2,128)(2,1)}, bf16[2,128,2,8]{3,2,0,1:T(2,128)(2,1)}, u32[]{:S(2)}, u32[]{:S(2)}) collective-permute-start(bf16[2,128,2,8]{3,2,0,1:T(2,128)(2,1)} %get-tuple-element.49), channel_id=1, source_target_pairs={{0,16},{4,20},{8,24},{12,28},{16,0},{20,4},{24,8},{28,12},{1,17},{... | collective-permute-start | bytes 24584 | tf_op jit(solution)/shard_map/ppermute | solution.py:123
  524.0 20.2 %collective-permute-start.19 = (bf16[2,128,2,8]{3,2,0,1:T(2,128)(2,1)}, bf16[2,128,2,8]{3,2,0,1:T(2,128)(2,1)}, u32[]{:S(2)}, u32[]{:S(2)}) collective-permute-start(bf16[2,128,2,8]{3,2,0,1:T(2,128)(2,1)} %get-tuple-element.48), channel_id=1, source_target_pairs={{0,20},{4,16},{8,28},{12,24},{16,4},{20,0},{24,12},{28,8},{1,21},{... | collective-permute-start | bytes 24584 | tf_op jit(solution)/shard_map/ppermute | solution.py:123
  525.5 19.7 %collective-permute-start.20 = (bf16[2,128,2,8]{3,2,0,1:T(2,128)(2,1)}, bf16[2,128,2,8]{3,2,0,1:T(2,128)(2,1)}, u32[]{:S(2)}, u32[]{:S(2)}) collective-permute-start(bf16[2,128,2,8]{3,2,0,1:T(2,128)(2,1)} %get-tuple-element.47), channel_id=1, source_target_pairs={{0,24},{4,28},{8,16},{12,20},{16,8},{20,12},{24,0},{28,4},{1,25},{... | collective-permute-start | bytes 24584 | tf_op jit(solution)/shard_map/ppermute | solution.py:123
  529.9 16.3 %collective-permute-start.21 = (bf16[2,128,2,8]{3,2,0,1:T(2,128)(2,1)}, bf16[2,128,2,8]{3,2,0,1:T(2,128)(2,1)}, u32[]{:S(2)}, u32[]{:S(2)}) collective-permute-start(bf16[2,128,2,8]{3,2,0,1:T(2,128)(2,1)} %get-tuple-element.46), channel_id=1, source_target_pairs={{0,28},{4,24},{8,20},{12,16},{16,12},{20,8},{24,4},{28,0},{1,29},{... | collective-permute-start | bytes 24584 | tf_op jit(solution)/shard_map/ppermute | solution.py:123
  567.7 5.9 %collective-permute-start.22 = (bf16[1,10752]{1,0:T(2,128)(2,1)S(1)}, bf16[1,10752]{1,0:T(2,128)(2,1)S(1)}, u32[]{:S(2)}, u32[]{:S(2)}) collective-permute-start(bf16[1,10752]{1,0:T(2,128)(2,1)S(1)} %slice.274), channel_id=1, source_target_pairs={{4,0},{8,4},{12,8},{16,12},{20,16},{24,20},{28,24},{5,1},{9,5},{13... | collective-permute-start | bytes 64520 | tf_op jit(solution)/shard_map/ppermute | solution.py:18
  575.1 4.8 collective-permute-start.23
Sparse Core Ops, SparseCore 0:
  339.2 28.9 all-reduce.4
  485.0 28.2 all-reduce.6
